TPU v7x, 32 devices: a whole 2x2x4 slice. The times are simulated.
32 devices in a mesh: groups: 2 (over x), tm: 16 (over z, y, core).
Axes of the slice: x: 2, y: 2, z: 4, core: 2. Of those that a mesh axis runs over, the one named last changes fastest.
Arguments:
- new_rows: bfloat16 [16384, 2048], P(('groups', 'tm')), parts along dimension 0, may hold values from -6 to 6
- w_query: bfloat16 [2048, 1024], replicated, may hold values from -0.125 to 0.125
- w_out: bfloat16 [1024, 2048], replicated, may hold values from -1.5 to 1.5
- base_kv: bfloat16 [2, 128, 128, 1024], P(None, ('groups', 'tm')), parts along dimension 1, may hold values from -1400 to 1400
- slopes: float32 [8], replicated, may hold values from 0.05 to 2
- row_owner: int32 [16384, 1], P(('groups', 'tm')), parts along dimension 0, may hold values from 0 to 15; in each aligned block of 512 rows (0 to 511, 512 to 1023, ...) at most 64 rows name the same one
- row_position: int32 [16384], P(('groups', 'tm')), parts along dimension 0, may hold values from 0 to 11
- row_reach: int32 [16384, 2], P(('groups', 'tm')), parts along dimension 0, may hold values from 0 to 2
Outputs:
- upsampled: bfloat16 [16384, 2048], P(('groups', 'tm')), parts along dimension 0
There are 2 independent parts, one for each index of `groups`. A program takes and returns all parts, laid end to end along the dimension named above; an argument that names none is the same for every part. Nothing has to cross between parts.
Inputs may be any that keep to these rules, and one draw needn't show every extreme that they name: `row_owner`: in the rows of one time block no owner is named by more than 64 rows, a bound that some block reaches.
All inputs are finite; a program needn't handle non-finite values.
Results may differ from a plain program's by a relative error of at most 0.01.
The roundings to bfloat16 on the way count: a program that leaves them out, or rounds other values in their place, can miss the bound.
Values may be sent and summed in bfloat16 or wider, within the bound.
A program may use at most 128 MiB of HBM per device.

v0:
```python
import jax
import jax.numpy as jnp
from jax import lax
from jax.sharding import PartitionSpec as P

HEADS = 8
HEAD_DIM = 128
REACH = 2


def padded(block, sides, width):
    for axis, dim in sides:
        count = lax.axis_size(axis)
        forward = [(i, i + 1) for i in range(count - 1)]
        backward = [(target, source) for source, target in forward]
        low = lax.ppermute(
            lax.slice_in_dim(block, block.shape[dim] - width, None, axis=dim), axis, forward
        )
        high = lax.ppermute(lax.slice_in_dim(block, 0, width, axis=dim), axis, backward)
        block = jnp.concatenate([low, block, high], axis=dim)
    return block


def attend(queries, details, extended, slopes, first_frame, total_frames):
    slots = queries.shape[0]
    frames = extended.shape[1]
    tile = extended.shape[2]
    position = details[:, 0]
    centre = first_frame + REACH + position // 3
    moment = centre.astype(jnp.float32) + (position % 3 + 1).astype(jnp.float32) * 0.25
    key_frame = jnp.repeat(first_frame + jnp.arange(frames, dtype=jnp.int32), tile)
    allowed = (key_frame[None, :] >= (centre - details[:, 1])[:, None]) & (
        key_frame[None, :] <= (centre + details[:, 2])[:, None]
    )
    allowed = allowed & (key_frame >= 0)[None, :] & (key_frame < total_frames)[None, :]
    distance = jnp.abs(key_frame.astype(jnp.float32)[None, None, :] - moment[None, :, None])
    query_heads = queries.reshape(slots, HEADS, HEAD_DIM)
    key_heads = extended[0].reshape(frames * tile, HEADS, HEAD_DIM)
    value_heads = extended[1].reshape(frames * tile, HEADS, HEAD_DIM)
    scores = jnp.einsum(
        "shd,khd->hsk", query_heads, key_heads, preferred_element_type=jnp.float32
    ) * (1.0 / HEAD_DIM**0.5)
    scores = scores - slopes[:, None, None] * distance
    scores = jnp.where(allowed[None], scores, -1e30)
    largest = jnp.max(scores, axis=-1, keepdims=True)
    raised = jnp.exp(scores - largest)
    weights = (raised / jnp.sum(raised, axis=-1, keepdims=True)).astype(jnp.bfloat16)
    attended = jnp.einsum("hsk,khd->shd", weights, value_heads, preferred_element_type=jnp.float32)
    return attended.reshape(slots, HEADS * HEAD_DIM).astype(jnp.bfloat16)


def per_device(new_rows, w_query, w_out, base_kv, slopes, row_owner, row_position, row_reach):
    devices = lax.axis_size("tm")
    rows = new_rows.shape[0]
    capacity = 2 * rows // devices
    frames = base_kv.shape[1]
    extended = padded(base_kv, (("tm", 1),), REACH)
    first_frame = lax.axis_index("tm") * frames - REACH
    total_frames = frames * devices
    owner = row_owner[:, 0]
    owner_hits = (owner[:, None] == jnp.arange(devices, dtype=jnp.int32)[None, :]).astype(jnp.int32)
    owner_rank = jnp.cumsum(owner_hits, axis=0) - 1
    slot_index = owner * capacity + jnp.sum(owner_hits * owner_rank, axis=1)
    row_info = jnp.stack([row_position, row_reach[:, 0], row_reach[:, 1]], axis=1)
    info_buffer = (
        jnp.zeros((devices * capacity, 3), jnp.int32)
        .at[slot_index]
        .set(row_info)
        .reshape(devices, capacity, 3)
    )
    queries = jnp.dot(new_rows, w_query, preferred_element_type=jnp.float32).astype(jnp.bfloat16)
    query_buffer = (
        jnp.zeros((devices * capacity, queries.shape[1]), jnp.bfloat16).at[slot_index].set(queries)
    )
    query_buffer = query_buffer.reshape(devices, capacity, queries.shape[1])
    received = lax.all_to_all(query_buffer, "tm", split_axis=0, concat_axis=0, tiled=True)
    details = lax.all_to_all(info_buffer, "tm", split_axis=0, concat_axis=0, tiled=True)
    sources = received.shape[0]
    items = received.shape[1]
    attended = attend(
        received.reshape(sources * items, -1),
        details.reshape(sources * items, 3),
        extended,
        slopes,
        first_frame,
        total_frames,
    )
    returned = lax.all_to_all(
        attended.reshape(sources, items, -1), "tm", split_axis=0, concat_axis=0, tiled=True
    )
    gathered = returned.reshape(devices * capacity, -1)[slot_index]
    return jnp.dot(gathered, w_out, preferred_element_type=jnp.float32).astype(jnp.bfloat16)


def solution(mesh):
    return jax.shard_map(
        per_device,
        mesh=mesh,
        in_specs=(
            P(("groups", "tm"), None),
            P(),
            P(),
            P(None, ("groups", "tm"), None, None),
            P(),
            P(("groups", "tm"), None),
            P(("groups", "tm")),
            P(("groups", "tm"), None),
        ),
        out_specs=P(("groups", "tm"), None),
        check_vma=False,
    )
```

profile of v0, /device:TPU:13, one launch (start us, length us, event | category | flops | bytes accessed | tf_op | source)
XLA Modules:
  0.0 206.4 jit_solution(8815354988031635215)
XLA Ops:
  0.0 0.0 copy-start
  0.0 0.8 fusion.44
  0.8 1.1 reduce-window.6
  2.0 0.2 slice_reduce_fusion
  2.2 0.8 fusion.43
  3.0 0.7 compare_select_fusion
  3.7 0.7 pad_add_fusion
  4.4 0.1 copy.30
  4.6 1.8 scatter_custom_fusion
  6.4 0.2 copy.31
  6.6 0.7 reshape.253
  7.3 6.6 %all-to-all-start = ((s32[16,1,192]{2,1,0:T(1,128)}), s32[16,1,192]{2,1,0:T(1,128)S(1)}, u32[]{:S(2)}, u32[]{:S(2)}) async-start(s32[16,1,192]{2,1,0:T(1,128)} %reshape.253), calls=%async_computation | async-start | bytes 32768 | tf_op jit(solution)/shard_map/all_to_all | solution.py:77
  13.9 0.0 copy-done
  13.9 4.5 %convolution_convert_fusion.1 = bf16[512,1024]{1,0:T(8,128)(2,1)S(1)} fusion(bf16[512,2048]{1,0:T(8,128)(2,1)S(1)} %copy-done, bf16[2048,1024]{1,0:T(8,128)(2,1)} %param.9), kind=kOutput, calls=%fused_computation.27 | convolution fusion | flops 2148007936 | bytes 7340032 | tf_op jit(solution)/shard_map/dot_general | solution.py:71
  18.4 4.1 %scatter_custom_fusion.1 = bf16[1024,1024]{1,0:T(8,128)(2,1)} fusion(s32[512]{0:T(512)S(1)} %bitcast.73, bf16[512,1024]{1,0:T(8,128)(2,1)S(1)} %convolution_convert_fusion.1, bf16[]{:T(256)} %constant.52.clone.1), kind=kCustom, calls=%fused_computation.28 | custom fusion | bytes 2097154 | tf_op jit(solution)/shard_map/scatter | solution.py:73
  22.6 0.0 all-to-all-done
  22.6 6.0 %all-to-all-start.1 = ((bf16[16,64,1024]{2,1,0:T(8,128)(2,1)}), bf16[16,64,1024]{2,1,0:T(8,128)(2,1)}, u32[]{:S(2)}, u32[]{:S(2)}) async-start(bf16[16,64,1024]{2,1,0:T(8,128)(2,1)} %bitcast.55), calls=%async_computation.1 | async-start | bytes 4194304 | tf_op jit(solution)/shard_map/all_to_all | solution.py:76
  28.6 3.1 %fusion.61 = (bf16[2,2,128,1024]{3,2,1,0:T(8,128)(2,1)}, bf16[2,2,128,1024]{3,2,1,0:T(8,128)(2,1)}) fusion(bf16[2,4,128,1024]{3,2,1,0:T(8,128)(2,1)} %param.11), kind=kLoop, calls=%fused_computation.72 | loop fusion | bytes 4194304 | tf_op jit(solution)/shard_map/slice | solution.py:19
  31.7 2.3 %collective-permute-start.1 = (bf16[2,2,128,1024]{3,2,1,0:T(8,128)(2,1)}, bf16[2,2,128,1024]{3,2,1,0:T(8,128)(2,1)S(1)}, u32[]{:S(2)}, u32[]{:S(2)}) collective-permute-start(bf16[2,2,128,1024]{3,2,1,0:T(8,128)(2,1)} %get-tuple-element.10), channel_id=1, source_target_pairs={{1,0},{2,1},{3,2},{4,3},{5,4},{6,5},{7,6},{8,7},{9,8},{10,9},{11,1... | collective-permute-start | bytes 3145736 | tf_op jit(solution)/shard_map/ppermute | solution.py:19
  34.0 4.4 %collective-permute-start = (bf16[2,2,128,1024]{3,2,1,0:T(8,128)(2,1)}, bf16[2,2,128,1024]{3,2,1,0:T(8,128)(2,1)}, u32[]{:S(2)}, u32[]{:S(2)}) collective-permute-start(bf16[2,2,128,1024]{3,2,1,0:T(8,128)(2,1)} %get-tuple-element.11), channel_id=1, source_target_pairs={{0,1},{1,2},{2,3},{3,4},{4,5},{5,6},{6,7},{7,8},{8,9},{9,10},{10,1... | collective-permute-start | bytes 3145736 | tf_op jit(solution)/shard_map/ppermute | solution.py:16
  38.4 0.1 bitcast_compare_fusion.1
  38.5 0.1 broadcast_bitcast_fusion
  38.5 0.6 broadcast.208
  39.1 0.7 reduce.4
  39.9 0.1 reshape.254
  39.9 0.1 reshape.219
  40.0 0.0 copy-start.1
  40.1 2.3 %subtract_abs_fusion = f32[1024,1024]{0,1:T(8,128)} fusion(f32[1024]{0:T(1024)S(1)} %fusion.47, f32[1024]{0:T(1024)S(1)} %get-tuple-element.17), kind=kLoop, calls=%fused_computation.14 | loop fusion | flops 2097152 | bytes 4202496 | tf_op jit(solution)/shard_map/abs | solution.py:36
  42.4 2.2 %and_and_fusion = pred[1024,1024]{0,1:T(8,128)(4,1)} fusion(s32[1024]{0:T(1024)S(1)} %bitcast.68, s32[1024]{0:T(1024)S(1)} %bitcast.69, s32[1024]{0:T(1024)S(1)} %get-tuple-element.16, pred[1024]{0:T(1024)(128)(4,1)S(1)} %get-tuple-element.15, pred[1024]{0:T(1024)(128)(4,1)S(1)} %get-tuple-element.14), kind=kLoop, calls=%fused_computation.15 | loop fusion | flops 5242880 | bytes 1062912 | tf_op jit(solution)/shard_map/and | solution.py:35
  44.6 41.1 %collective-permute-done = bf16[2,2,128,1024]{3,2,1,0:T(8,128)(2,1)} collective-permute-done((bf16[2,2,128,1024]{3,2,1,0:T(8,128)(2,1)}, bf16[2,2,128,1024]{3,2,1,0:T(8,128)(2,1)}, u32[]{:S(2)}, u32[]{:S(2)}) %collective-permute-start) | collective-permute-done | bytes 1048608 | tf_op jit(solution)/shard_map/ppermute | solution.py:16
  85.7 1.3 constant_dynamic-update-slice_fusion.2
  87.0 0.0 copy-done.1
  87.0 0.2 constant_dynamic-update-slice_fusion.1
  87.2 0.0 collective-permute-done.1
  87.2 0.1 constant_dynamic-update-slice_fusion
  87.3 0.6 fusion.60
  88.0 2.0 copy.40
  90.0 0.0 copy-start.2
  90.0 0.0 copy-start.3
  90.0 1.9 copy.42
  91.9 0.0 all-to-all-done.1
  91.9 3.6 %copy.41 = bf16[128,8,8,128]{3,2,1,0:T(8,128)(2,1)} copy(bf16[128,8,8,128]{3,1,2,0:T(8,128)(2,1)} %bitcast.23) | data formatting | bytes 4194304
  95.5 0.0 copy-done.2
  95.5 0.0 copy-done.3
  95.5 15.8 %fusion.62 = f32[8,1024]{1,0:T(8,128)S(1)} fusion(f32[1024,1024]{0,1:T(8,128)} %subtract_abs_fusion, f32[8]{0:T(128)S(1)} %copy-done.3, pred[1024,1024]{0,1:T(8,128)(4,1)S(1)} %copy-done.2, bf16[1024,8,128]{2,1,0:T(8,128)(2,1)} %bitcast.59, bf16[1024,8,128]{2,1,0:T(8,128)(2,1)} %bitcast.61), kind=kOutput, calls=%fused_computation.73 | convolution fusion | flops 2197816320 | bytes 9469984 | tf_op jit(solution)/shard_map/sub | solution.py:46
  111.3 22.6 %convert_bitcast_fusion = bf16[1024,8,128]{0,2,1:T(8,128)(2,1)} fusion(f32[8,1024]{1,0:T(8,128)S(1)} %fusion.62, f32[1024,1024]{0,1:T(8,128)} %subtract_abs_fusion, f32[8]{0:T(128)S(1)} %copy-done.3, pred[1024,1024]{0,1:T(8,128)(4,1)S(1)} %copy-done.2, bf16[1024,8,128]{2,1,0:T(8,128)(2,1)} %bitcast.58, bf16[1024,8,128]{2,1,0:T(8,128)(2,1)} %bitcast.60, ...), kind=kOutput, calls=%fused_computation.19 | convolution fusion | flops 4354745344 | bytes 13664288 | tf_op jit(solution)/shard_map/hsk,khd->shd/dot_general | solution.py:48
  133.9 4.1 %copy.36 = bf16[1024,8,128]{2,1,0:T(8,128)(2,1)} copy(bf16[1024,8,128]{0,2,1:T(8,128)(2,1)} %convert_bitcast_fusion) | data formatting | bytes 4194304 | tf_op jit(solution)/shard_map/convert_element_type | solution.py:49
  138.1 4.2 %convert_element_type.53 = bf16[16,64,1024]{2,1,0:T(8,128)(2,1)} reshape(bf16[1024,8,128]{2,1,0:T(8,128)(2,1)} %copy.36) | data formatting | bytes 4194304 | tf_op jit(solution)/shard_map/convert_element_type | solution.py:49
  142.3 6.2 %all-to-all-start.2 = ((bf16[16,64,1024]{2,1,0:T(8,128)(2,1)}), bf16[16,64,1024]{2,1,0:T(8,128)(2,1)}, u32[]{:S(2)}, u32[]{:S(2)}) async-start(bf16[16,64,1024]{2,1,0:T(8,128)(2,1)} %convert_element_type.53), calls=%async_computation.2 | async-start | bytes 4194304 | tf_op jit(solution)/shard_map/all_to_all | solution.py:88
  148.4 47.5 %all-to-all-done.2 = bf16[16,64,1024]{2,1,0:T(8,128)(2,1)} async-done(((bf16[16,64,1024]{2,1,0:T(8,128)(2,1)}), bf16[16,64,1024]{2,1,0:T(8,128)(2,1)}, u32[]{:S(2)}, u32[]{:S(2)}) %all-to-all-start.2) | async-done | bytes 2097184 | tf_op jit(solution)/shard_map/all_to_all | solution.py:88
  195.9 4.6 %gather_fusion = bf16[512,1024]{1,0:T(8,128)(2,1)S(1)} fusion(bf16[1024,1024]{1,0:T(8,128)(2,1)} %bitcast.14, s32[1024]{0:T(1024)S(1)} %pad_clamp_fusion), kind=kCustom, calls=%fused_computation | custom fusion | bytes 2099200 | tf_op jit(solution)/shard_map/gather | solution.py:91
  200.5 5.8 %convolution_convert_fusion = bf16[512,2048]{1,0:T(8,128)(2,1)} fusion(bf16[512,1024]{1,0:T(8,128)(2,1)S(1)} %gather_fusion, bf16[1024,2048]{1,0:T(8,128)(2,1)} %param.10), kind=kOutput, calls=%fused_computation.17 | convolution fusion | flops 2148532224 | bytes 7340032 | tf_op jit(solution)/shard_map/dot_general | solution.py:92
  (9 shorter events, 0.1 us)
Async XLA Ops:
  0.0 13.9 %copy-start = (bf16[512,2048]{1,0:T(8,128)(2,1)S(1)}, bf16[512,2048]{1,0:T(8,128)(2,1)}, u32[]{:S(2)}) copy-start(bf16[512,2048]{1,0:T(8,128)(2,1)} %param.8) | copy-start | bytes 6291460
  7.3 15.2 %all-to-all-start = ((s32[16,1,192]{2,1,0:T(1,128)}), s32[16,1,192]{2,1,0:T(1,128)S(1)}, u32[]{:S(2)}, u32[]{:S(2)}) async-start(s32[16,1,192]{2,1,0:T(1,128)} %reshape.253), calls=%async_computation | async-start | bytes 32768 | tf_op jit(solution)/shard_map/all_to_all | solution.py:77
  22.6 69.4 %all-to-all-start.1 = ((bf16[16,64,1024]{2,1,0:T(8,128)(2,1)}), bf16[16,64,1024]{2,1,0:T(8,128)(2,1)}, u32[]{:S(2)}, u32[]{:S(2)}) async-start(bf16[16,64,1024]{2,1,0:T(8,128)(2,1)} %bitcast.55), calls=%async_computation.1 | async-start | bytes 4194304 | tf_op jit(solution)/shard_map/all_to_all | solution.py:76
  31.7 55.5 %collective-permute-start.1 = (bf16[2,2,128,1024]{3,2,1,0:T(8,128)(2,1)}, bf16[2,2,128,1024]{3,2,1,0:T(8,128)(2,1)S(1)}, u32[]{:S(2)}, u32[]{:S(2)}) collective-permute-start(bf16[2,2,128,1024]{3,2,1,0:T(8,128)(2,1)} %get-tuple-element.10), channel_id=1, source_target_pairs={{1,0},{2,1},{3,2},{4,3},{5,4},{6,5},{7,6},{8,7},{9,8},{10,9},{11,1... | collective-permute-start | bytes 3145736 | tf_op jit(solution)/shard_map/ppermute | solution.py:19
  34.0 51.7 %collective-permute-start = (bf16[2,2,128,1024]{3,2,1,0:T(8,128)(2,1)}, bf16[2,2,128,1024]{3,2,1,0:T(8,128)(2,1)}, u32[]{:S(2)}, u32[]{:S(2)}) collective-permute-start(bf16[2,2,128,1024]{3,2,1,0:T(8,128)(2,1)} %get-tuple-element.11), channel_id=1, source_target_pairs={{0,1},{1,2},{2,3},{3,4},{4,5},{5,6},{6,7},{7,8},{8,9},{9,10},{10,1... | collective-permute-start | bytes 3145736 | tf_op jit(solution)/shard_map/ppermute | solution.py:16
  40.0 47.0 %copy-start.1 = (bf16[2,4,128,1024]{3,2,1,0:T(8,128)(2,1)S(1)}, bf16[2,4,128,1024]{3,2,1,0:T(8,128)(2,1)}, u32[]{:S(2)}) copy-start(bf16[2,4,128,1024]{3,2,1,0:T(8,128)(2,1)} %param.11) | copy-start | bytes 6291460
  90.0 5.5 %copy-start.2 = (pred[1024,1024]{0,1:T(8,128)(4,1)S(1)}, pred[1024,1024]{0,1:T(8,128)(4,1)}, u32[]{:S(2)}) copy-start(pred[1024,1024]{0,1:T(8,128)(4,1)} %and_and_fusion) | copy-start | bytes 3145732
  90.0 5.5 %copy-start.3 = (f32[8]{0:T(128)S(1)}, f32[8]{0:T(128)}, u32[]{:S(2)}) copy-start(f32[8]{0:T(128)} %param.12) | copy-start | bytes 100
  142.3 53.7 %all-to-all-start.2 = ((bf16[16,64,1024]{2,1,0:T(8,128)(2,1)}), bf16[16,64,1024]{2,1,0:T(8,128)(2,1)}, u32[]{:S(2)}, u32[]{:S(2)}) async-start(bf16[16,64,1024]{2,1,0:T(8,128)(2,1)} %convert_element_type.53), calls=%async_computation.2 | async-start | bytes 4194304 | tf_op jit(solution)/shard_map/all_to_all | solution.py:88
where the time goes:
time: 207 us; the launch traced here: 206 us
  waiting for transfers between devices  88.6 us (43%)
  matrix products  48.8 us (24%)
  local copies, waits for them, and re-layouts  33.9 us (16%)
  starting transfers between devices  25.4 us (12%)
  other arithmetic  9.64 us (5%)
    all_to_all x1, waiting for transfers between devices, per_device(): lax.all_to_all(attended.reshape(sources, items, -1), 'tm', split_axis=0,...  47.5 us
    ppermute x1, waiting for transfers between devices, padded(): lax.ppermute(lax.slice_in_dim(block, block.shape[dim] - width, None, axis...  41.1 us
    dot_general x1, matrix products, attend(): jnp.einsum('hsk,khd->shd', weights, value_heads, preferred_element_type=j...  22.6 us
    sub x1, matrix products, attend(): raised = jnp.exp(scores - largest)  15.8 us
    unnamed x15, local copies, waits for them, and re-layouts  9.88 us
    convert_element_type x2, local copies, waits for them, and re-layouts, attend(): return attended.reshape(slots, HEADS * HEAD_DIM).astype(jnp.bfloat16)  8.32 us
    all_to_all x1, starting transfers between devices, per_device(): lax.all_to_all(info_buffer, 'tm', split_axis=0, concat_axis=0, tiled=True)  6.55 us
    all_to_all x1, starting transfers between devices, per_device(): lax.all_to_all(attended.reshape(sources, items, -1), 'tm', split_axis=0,...  6.16 us
  transfers between devices with their start and end apart: 5, of which 2 were waited for; matrix products, arithmetic and copies ran while one was open for 12% of the time, Pallas kernels for 0%

commit v1 on v0

v1 whole, which is shorter than its diff:
```python
import functools

import jax
import jax.numpy as jnp
from jax import lax
from jax.experimental import pallas as pl
from jax.experimental.pallas import tpu as pltpu
from jax.sharding import PartitionSpec as P

HEAD_DIM = 128
REACH = 2
CHUNK = 128
MESH = pl.DeviceIdType.MESH
F32 = jnp.float32
BF16 = jnp.bfloat16


def iota(shape, axis):
    return lax.broadcasted_iota(jnp.int32, shape, axis)


def kernel(
    n, slopes_ref, info_ref, x_hbm, wq_hbm, wo_hbm, kv_hbm, out_ref,
    x, wq, wo, ext, queries, q_slots, q_recv, m_slots, m_recv, att, ret, vt, gather,
    load_sem, halo_send, halo_recv, qs_sem, qr_sem, ms_sem, mr_sem, rs_sem, rr_sem,
):
    me = lax.axis_index("tm")
    rows = x.shape[0]
    slots = q_slots.shape[0]
    cap = slots // n
    group = CHUNK // cap
    chunks = slots // CHUNK
    half = chunks // 2
    frames = kv_hbm.shape[1]
    wide = frames + 2 * REACH
    tokens = kv_hbm.shape[2]
    heads = queries.shape[1] // HEAD_DIM
    own = lax.div(me, group)
    own_half = lax.div(own, half)
    own_spot = lax.rem(own, half)

    loads = [
        pltpu.make_async_copy(kv_hbm, ext.at[:, REACH:REACH + frames], load_sem.at[0]),
        pltpu.make_async_copy(x_hbm, x, load_sem.at[1]),
        pltpu.make_async_copy(wq_hbm, wq, load_sem.at[2]),
        pltpu.make_async_copy(wo_hbm, wo, load_sem.at[3]),
    ]
    for load in loads:
        load.start()

    barrier = pltpu.get_barrier_semaphore()

    @pl.loop(1, n)
    def _(k):
        pl.semaphore_signal(
            barrier, inc=1, device_id={"tm": lax.rem(me + k, n)}, device_id_type=MESH
        )

    pl.semaphore_wait(barrier, n - 1)

    to_right = pltpu.make_async_remote_copy(
        src_ref=kv_hbm.at[:, frames - REACH:], dst_ref=ext.at[:, :REACH],
        send_sem=halo_send.at[0], recv_sem=halo_recv.at[0],
        device_id={"tm": lax.rem(me + 1, n)}, device_id_type=MESH,
    )
    to_left = pltpu.make_async_remote_copy(
        src_ref=kv_hbm.at[:, :REACH], dst_ref=ext.at[:, REACH + frames:],
        send_sem=halo_send.at[1], recv_sem=halo_recv.at[1],
        device_id={"tm": lax.rem(me + n - 1, n)}, device_id_type=MESH,
    )

    @pl.when(me < n - 1)
    def _():
        to_right.start()

    @pl.when(me > 0)
    def _():
        to_left.start()

    edge = jnp.zeros((2, REACH, tokens, ext.shape[3]), BF16)

    @pl.when(me == 0)
    def _():
        ext[:, :REACH] = edge

    @pl.when(me == n - 1)
    def _():
        ext[:, REACH + frames:] = edge

    info = info_ref[...]
    owner = info[0:1]
    hits = (owner == iota((n, rows), 0).astype(F32)).astype(F32)
    upper = (iota((rows, rows), 0) <= iota((rows, rows), 1)).astype(F32).astype(BF16)
    counts = jnp.dot(hits.astype(BF16), upper, preferred_element_type=F32)
    rank = jnp.sum(hits * counts, axis=0, keepdims=True) - 1.0
    slot = owner * float(cap) + rank
    slot_column = jnp.sum(
        jnp.where(iota((rows, rows), 0) == iota((rows, rows), 1), slot, 0.0), axis=1, keepdims=True
    )
    gather[...] = (slot_column == iota((rows, slots), 1).astype(F32)).astype(F32).astype(BF16)
    facts = info.astype(BF16)
    spot = rank + (lax.rem(me, group) * cap).astype(F32)

    loads[1].wait()
    loads[2].wait()

    @pl.loop(0, queries.shape[1] // 256)
    def _(j):
        columns = pl.ds(pl.multiple_of(j * 256, 256), 256)
        queries[:, columns] = jnp.dot(x[...], wq[:, columns], preferred_element_type=F32).astype(BF16)

    def q_copy(target, source):
        return pltpu.make_async_remote_copy(
            src_ref=q_slots.at[pl.ds(pl.multiple_of(target * cap, cap), cap)],
            dst_ref=q_recv.at[pl.ds(pl.multiple_of(source * cap, cap), cap)],
            send_sem=qs_sem.at[target], recv_sem=qr_sem.at[source],
            device_id={"tm": target}, device_id_type=MESH,
        )

    def m_copy(target, source):
        return pltpu.make_async_remote_copy(
            src_ref=m_slots.at[target], dst_ref=m_recv.at[source],
            send_sem=ms_sem.at[target], recv_sem=mr_sem.at[source],
            device_id={"tm": target}, device_id_type=MESH,
        )

    def r_copy(target, source):
        return pltpu.make_async_remote_copy(
            src_ref=att.at[pl.ds(pl.multiple_of(target * cap, cap), cap)],
            dst_ref=ret.at[pl.ds(pl.multiple_of(source * cap, cap), cap)],
            send_sem=rs_sem.at[target], recv_sem=rr_sem.at[source],
            device_id={"tm": target}, device_id_type=MESH,
        )

    mine = pl.ds(pl.multiple_of(me * cap, cap), cap)

    @pl.loop(0, chunks)
    def _(i):
        side = lax.rem(own_half + 1 + lax.rem(i, 2), 2)
        chunk = side * half + lax.rem(own_spot + lax.div(i, 2), half)
        first = (chunk * CHUNK).astype(F32)
        place = (slot - first == iota((CHUNK, rows), 0).astype(F32)).astype(F32).astype(BF16)

        @pl.loop(0, queries.shape[1] // 256)
        def _(j):
            columns = pl.ds(pl.multiple_of(j * 256, 256), 256)
            q_slots[pl.ds(pl.multiple_of(chunk * CHUNK, CHUNK), CHUNK), columns] = jnp.dot(
                place, queries[:, columns], preferred_element_type=F32
            ).astype(BF16)

        @pl.loop(0, group)
        def _(g):
            target = chunk * group + g
            lanes = jnp.where(owner == target.astype(F32), spot, -1.0)
            spread = (lanes == iota((CHUNK, rows), 0).astype(F32)).astype(F32).astype(BF16)
            m_slots[target] = lax.dot_general(
                facts, spread, (((1,), (1,)), ((), ())), preferred_element_type=F32
            )

            @pl.when(target != me)
            def _():
                m_copy(target, me).start()
                q_copy(target, me).start()

            @pl.when(target == me)
            def _():
                m_recv[target] = m_slots[target]
                q_recv[mine] = q_slots[mine]

    def turn(f):
        @pl.loop(0, heads)
        def _(h):
            columns = pl.ds(pl.multiple_of(h * HEAD_DIM, HEAD_DIM), HEAD_DIM)
            vt[columns, pl.ds(pl.multiple_of(f * tokens, tokens), tokens)] = (
                ext[1, f, :, columns].astype(F32).T.astype(BF16)
            )

    loads[0].wait()

    @pl.loop(REACH, REACH + frames)
    def _(f):
        turn(f)

    @pl.when(me > 0)
    def _():
        to_right.wait_recv()

    @pl.when(me < n - 1)
    def _():
        to_left.wait_recv()

    @pl.loop(0, REACH)
    def _(f):
        turn(f)
        turn(REACH + frames + f)

    first_frame = (me * frames - REACH).astype(F32)

    @pl.loop(0, chunks)
    def _(i):
        side = lax.rem(own_half + lax.rem(i, 2), 2)
        chunk = side * half + lax.rem(own_spot + half - lax.div(i, 2), half)

        @pl.loop(0, group)
        def _(g):
            source = chunk * group + g

            @pl.when(source != me)
            def _():
                m_copy(me, source).wait_recv()
                q_copy(me, source).wait_recv()

        told = m_recv[chunk * group]
        for g in range(1, group):
            told = told + m_recv[chunk * group + g]
        position = told[1:2].astype(jnp.int32)
        ahead = lax.div(position, 3)
        centre = (ahead + REACH).astype(F32) + first_frame
        moment = centre + (position - 3 * ahead + 1).astype(F32) * 0.25
        frame = first_frame + iota((wide, CHUNK), 0).astype(F32)
        allowed = (frame >= centre - told[2:3]) & (frame <= centre + told[3:4])
        allowed = allowed & (frame >= 0.0) & (frame < float(frames * n))
        distance = jnp.abs(frame - moment)
        chunk_rows = pl.ds(pl.multiple_of(chunk * CHUNK, CHUNK), CHUNK)

        @pl.loop(0, heads)
        def _(h):
            columns = pl.ds(pl.multiple_of(h * HEAD_DIM, HEAD_DIM), HEAD_DIM)
            bias = jnp.where(allowed, -slopes_ref[h] * distance, -1e30)
            keys = ext[0, :, :, columns].reshape(wide * tokens, HEAD_DIM)
            scores = lax.dot_general(
                keys, q_recv[chunk_rows, columns], (((1,), (1,)), ((), ())),
                preferred_element_type=F32,
            )
            scores = scores.reshape(wide, tokens, CHUNK) * (1.0 / HEAD_DIM**0.5) + bias[:, None, :]
            largest = jnp.max(jnp.max(scores, axis=0), axis=0, keepdims=True)
            raised = jnp.exp(scores - largest[None])
            total = jnp.sum(jnp.sum(raised, axis=0), axis=0, keepdims=True)
            weights = (raised * (1.0 / total)[None]).astype(BF16).reshape(wide * tokens, CHUNK)
            attended = jnp.dot(vt[columns, :], weights, preferred_element_type=F32)
            att[chunk_rows, columns] = attended.T.astype(BF16)

        @pl.loop(0, group)
        def _(g):
            source = chunk * group + g

            @pl.when(source != me)
            def _():
                r_copy(source, me).start()

            @pl.when(source == me)
            def _():
                ret[mine] = att[mine]

    loads[3].wait()

    @pl.loop(1, n)
    def _(k):
        r_copy(me, lax.rem(me + k, n)).wait_recv()

    @pl.loop(0, queries.shape[1] // 256)
    def _(j):
        columns = pl.ds(pl.multiple_of(j * 256, 256), 256)
        queries[:, columns] = jnp.dot(
            gather[...], ret[:, columns], preferred_element_type=F32
        ).astype(BF16)

    @pl.loop(0, wo.shape[1] // 256)
    def _(j):
        columns = pl.ds(pl.multiple_of(j * 256, 256), 256)
        out_ref[:, columns] = jnp.dot(
            queries[...], wo[:, columns], preferred_element_type=F32
        ).astype(BF16)

    @pl.loop(1, n)
    def _(k):
        target = lax.rem(me + k, n)
        m_copy(target, me).wait_send()
        q_copy(target, me).wait_send()
        r_copy(target, me).wait_send()

    @pl.when(me < n - 1)
    def _():
        to_right.wait_send()

    @pl.when(me > 0)
    def _():
        to_left.wait_send()


def per_device(n, new_rows, w_query, w_out, base_kv, slopes, row_owner, row_position, row_reach):
    rows, width = new_rows.shape
    features = w_query.shape[1]
    slots = 2 * rows
    frames, tokens = base_kv.shape[1:3]
    wide = frames + 2 * REACH
    info = jnp.concatenate(
        [row_owner.T, row_position[None], row_reach.T, jnp.zeros((4, rows), jnp.int32)], axis=0
    ).astype(F32)
    anywhere = pl.BlockSpec(memory_space=pl.ANY)
    return pl.pallas_call(
        functools.partial(kernel, n),
        out_shape=jax.ShapeDtypeStruct((rows, w_out.shape[1]), BF16),
        in_specs=[
            pl.BlockSpec(memory_space=pltpu.SMEM),
            pl.BlockSpec(memory_space=pltpu.VMEM),
            anywhere, anywhere, anywhere, anywhere,
        ],
        out_specs=pl.BlockSpec(memory_space=pltpu.VMEM),
        scratch_shapes=[
            pltpu.VMEM((rows, width), BF16),
            pltpu.VMEM(w_query.shape, BF16),
            pltpu.VMEM(w_out.shape, BF16),
            pltpu.VMEM((2, wide, tokens, features), BF16),
            pltpu.VMEM((rows, features), BF16),
            pltpu.VMEM((slots, features), BF16),
            pltpu.VMEM((slots, features), BF16),
            pltpu.VMEM((n, 8, CHUNK), F32),
            pltpu.VMEM((n, 8, CHUNK), F32),
            pltpu.VMEM((slots, features), BF16),
            pltpu.VMEM((slots, features), BF16),
            pltpu.VMEM((features, wide * tokens), BF16),
            pltpu.VMEM((rows, slots), BF16),
            pltpu.SemaphoreType.DMA((4,)),
            pltpu.SemaphoreType.DMA((2,)),
            pltpu.SemaphoreType.DMA((2,)),
            pltpu.SemaphoreType.DMA((n,)),
            pltpu.SemaphoreType.DMA((n,)),
            pltpu.SemaphoreType.DMA((n,)),
            pltpu.SemaphoreType.DMA((n,)),
            pltpu.SemaphoreType.DMA((n,)),
            pltpu.SemaphoreType.DMA((n,)),
        ],
        compiler_params=pltpu.CompilerParams(
            collective_id=0, has_side_effects=True, vmem_limit_bytes=48 * 1024 * 1024
        ),
        cost_estimate=pl.CostEstimate(
            flops=12 * 10**9, bytes_accessed=16 * 2**20, transcendentals=8 * 2**20
        ),
    )(slopes, info, new_rows, w_query, w_out, base_kv)


def solution(mesh):
    return jax.shard_map(
        functools.partial(per_device, mesh.shape["tm"]),
        mesh=mesh,
        in_specs=(
            P(("groups", "tm"), None),
            P(),
            P(),
            P(None, ("groups", "tm"), None, None),
            P(),
            P(("groups", "tm"), None),
            P(("groups", "tm")),
            P(("groups", "tm"), None),
        ),
        out_specs=P(("groups", "tm"), None),
        check_vma=False,
    )
```

time: 207 us -> 122 us (0.59)
  the two profiles are of different devices: /device:TPU:13 before, /device:TPU:5 now
where the time goes in v1:
time: 122 us; the launch traced here: 121 us
  Pallas kernels  117 us (96%)
  local copies, waits for them, and re-layouts  3.65 us (3%)
    pallas_call x1, Pallas kernels, per_device(): pl.pallas_call(functools.partial(kernel, n), out_shape=jax.ShapeDtypeStru...  117 us
    unnamed x5, local copies, waits for them, and re-layouts  3.57 us

profile of v1, /device:TPU:5, one launch (start us, length us, event | category | flops | bytes accessed | tf_op | source)
XLA Modules:
  0.0 121.3 jit_solution(10496184204118943857)
XLA Ops:
  0.0 0.1 pad.3.clone
  0.1 0.8 add_convert_fusion.info_ref
  0.9 0.0 copy-start
  0.9 1.6 %copy-done = bf16[512,2048]{1,0:T(8,128)(2,1)S(1)} copy-done((bf16[512,2048]{1,0:T(8,128)(2,1)S(1)}, bf16[512,2048]{1,0:T(8,128)(2,1)}, u32[]{:S(2)}) %copy-start) | copy-done | bytes 2097176
  2.5 0.0 copy-start.1
  2.5 0.7 copy-done.1
  3.1 116.9 %shard_map.82 = bf16[512,2048]{1,0:T(8,128)(2,1)S(1)} custom-call(f32[8]{0:T(128)S(1)} %copy-done.1, f32[8,512]{1,0:T(8,128)S(1)} %add_convert_fusion.info_ref, bf16[512,2048]{1,0:T(8,128)(2,1)S(1)} %copy-done, bf16[2048,1024]{1,0:T(8,128)(2,1)} %wq_hbm.1, bf16[1024,2048]{1,0:T(8,128)(2,1)} %wo_hbm.1, bf16[2,4,128,1024]{3,2,1,0:T(8,128)(2,1)} %kv_hbm.1), custom_call_target="tpu_custom_call" | custom-call | flops 12000000000 | bytes 16777216 | tf_op jit(solution)/shard_map/pallas_call | solution.py:301
  120.0 1.3 %copy.10 = bf16[512,2048]{1,0:T(8,128)(2,1)} copy(bf16[512,2048]{1,0:T(8,128)(2,1)S(1)} %shard_map.82) | data formatting | bytes 4194304
  (1 shorter events, 0.0 us)
Async XLA Ops:
  0.9 1.6 %copy-start = (bf16[512,2048]{1,0:T(8,128)(2,1)S(1)}, bf16[512,2048]{1,0:T(8,128)(2,1)}, u32[]{:S(2)}) copy-start(bf16[512,2048]{1,0:T(8,128)(2,1)} %x_hbm.1) | copy-start | bytes 6291460
  2.5 0.7 copy-start.1

commit v2 on v1

--- a/solution.py
+++ b/solution.py
@@ -20,9 +20,9 @@
 
 
 def kernel(
-    n, slopes_ref, info_ref, x_hbm, wq_hbm, wo_hbm, kv_hbm, out_ref,
-    x, wq, wo, ext, queries, q_slots, q_recv, m_slots, m_recv, att, ret, vt, gather,
-    load_sem, halo_send, halo_recv, qs_sem, qr_sem, ms_sem, mr_sem, rs_sem, rr_sem,
+    n, slopes_ref, info_ref, x_hbm, wq_hbm, wo_hbm, kv_hbm, out_hbm,
+    x, wq, wo, ext, queries, q_slots, q_recv, m_slots, m_recv, att, ret, vt, gather, out,
+    load_sem, wq_sem, out_sem, halo_send, halo_recv, qs_sem, qr_sem, ms_sem, mr_sem, rs_sem, rr_sem,
 ):
     me = lax.axis_index("tm")
     rows = x.shape[0]
@@ -39,15 +39,6 @@
     own_half = lax.div(own, half)
     own_spot = lax.rem(own, half)
 
-    loads = [
-        pltpu.make_async_copy(kv_hbm, ext.at[:, REACH:REACH + frames], load_sem.at[0]),
-        pltpu.make_async_copy(x_hbm, x, load_sem.at[1]),
-        pltpu.make_async_copy(wq_hbm, wq, load_sem.at[2]),
-        pltpu.make_async_copy(wo_hbm, wo, load_sem.at[3]),
-    ]
-    for load in loads:
-        load.start()
-
     barrier = pltpu.get_barrier_semaphore()
 
     @pl.loop(1, n)
@@ -55,6 +46,20 @@
         pl.semaphore_signal(
             barrier, inc=1, device_id={"tm": lax.rem(me + k, n)}, device_id_type=MESH
         )
+
+    load_x = pltpu.make_async_copy(x_hbm, x, load_sem.at[0])
+    load_kv = pltpu.make_async_copy(kv_hbm, ext.at[:, REACH:REACH + frames], load_sem.at[1])
+    load_wo = pltpu.make_async_copy(wo_hbm, wo, load_sem.at[2])
+
+    def load_wq(j):
+        columns = pl.ds(pl.multiple_of(j * 256, 256), 256)
+        return pltpu.make_async_copy(wq_hbm.at[:, columns], wq.at[:, columns], wq_sem.at[j])
+
+    load_x.start()
+
+    @pl.loop(0, wq.shape[1] // 256)
+    def _(j):
+        load_wq(j).start()
 
     pl.semaphore_wait(barrier, n - 1)
 
@@ -77,6 +82,7 @@
     def _():
         to_left.start()
 
+    load_kv.start()
     edge = jnp.zeros((2, REACH, tokens, ext.shape[3]), BF16)
 
     @pl.when(me == 0)
@@ -101,11 +107,11 @@
     facts = info.astype(BF16)
     spot = rank + (lax.rem(me, group) * cap).astype(F32)
 
-    loads[1].wait()
-    loads[2].wait()
+    load_x.wait()
 
     @pl.loop(0, queries.shape[1] // 256)
     def _(j):
+        load_wq(j).wait()
         columns = pl.ds(pl.multiple_of(j * 256, 256), 256)
         queries[:, columns] = jnp.dot(x[...], wq[:, columns], preferred_element_type=F32).astype(BF16)
 
@@ -136,8 +142,8 @@
 
     @pl.loop(0, chunks)
     def _(i):
-        side = lax.rem(own_half + 1 + lax.rem(i, 2), 2)
-        chunk = side * half + lax.rem(own_spot + lax.div(i, 2), half)
+        side = lax.rem(own_half + 1 + lax.div(i, half), 2)
+        chunk = side * half + lax.rem(own_spot + lax.rem(i, half), half)
         first = (chunk * CHUNK).astype(F32)
         place = (slot - first == iota((CHUNK, rows), 0).astype(F32)).astype(F32).astype(BF16)
 
@@ -175,7 +181,8 @@
                 ext[1, f, :, columns].astype(F32).T.astype(BF16)
             )
 
-    loads[0].wait()
+    load_wo.start()
+    load_kv.wait()
 
     @pl.loop(REACH, REACH + frames)
     def _(f):
@@ -223,7 +230,7 @@
         distance = jnp.abs(frame - moment)
         chunk_rows = pl.ds(pl.multiple_of(chunk * CHUNK, CHUNK), CHUNK)
 
-        @pl.loop(0, heads)
+        @pl.loop(0, heads, unroll=2)
         def _(h):
             columns = pl.ds(pl.multiple_of(h * HEAD_DIM, HEAD_DIM), HEAD_DIM)
             bias = jnp.where(allowed, -slopes_ref[h] * distance, -1e30)
@@ -252,25 +259,45 @@
             def _():
                 ret[mine] = att[mine]
 
-    loads[3].wait()
-
-    @pl.loop(1, n)
-    def _(k):
-        r_copy(me, lax.rem(me + k, n)).wait_recv()
-
-    @pl.loop(0, queries.shape[1] // 256)
-    def _(j):
+    queries[...] = jnp.zeros(queries.shape, BF16)
+
+    @pl.loop(0, chunks)
+    def _(i):
+        side = lax.rem(own_half + lax.div(i, half), 2)
+        chunk = side * half + lax.rem(own_spot + lax.rem(i, half), half)
+
+        @pl.loop(0, group)
+        def _(g):
+            source = chunk * group + g
+
+            @pl.when(source != me)
+            def _():
+                r_copy(me, source).wait_recv()
+
+        chunk_rows = pl.ds(pl.multiple_of(chunk * CHUNK, CHUNK), CHUNK)
+        for j in range(queries.shape[1] // 256):
+            columns = pl.ds(j * 256, 256)
+            queries[:, columns] += jnp.dot(
+                gather[:, chunk_rows], ret[chunk_rows, columns], preferred_element_type=F32
+            ).astype(BF16)
+
+    load_wo.wait()
+
+    def write(j):
         columns = pl.ds(pl.multiple_of(j * 256, 256), 256)
-        queries[:, columns] = jnp.dot(
-            gather[...], ret[:, columns], preferred_element_type=F32
-        ).astype(BF16)
+        return pltpu.make_async_copy(out.at[:, columns], out_hbm.at[:, columns], out_sem.at[j])
 
     @pl.loop(0, wo.shape[1] // 256)
     def _(j):
         columns = pl.ds(pl.multiple_of(j * 256, 256), 256)
-        out_ref[:, columns] = jnp.dot(
+        out[:, columns] = jnp.dot(
             queries[...], wo[:, columns], preferred_element_type=F32
         ).astype(BF16)
+        write(j).start()
+
+    @pl.loop(0, wo.shape[1] // 256)
+    def _(j):
+        write(j).wait()
 
     @pl.loop(1, n)
     def _(k):
@@ -306,7 +333,7 @@
             pl.BlockSpec(memory_space=pltpu.VMEM),
             anywhere, anywhere, anywhere, anywhere,
         ],
-        out_specs=pl.BlockSpec(memory_space=pltpu.VMEM),
+        out_specs=anywhere,
         scratch_shapes=[
             pltpu.VMEM((rows, width), BF16),
             pltpu.VMEM(w_query.shape, BF16),
@@ -321,7 +348,10 @@
             pltpu.VMEM((slots, features), BF16),
             pltpu.VMEM((features, wide * tokens), BF16),
             pltpu.VMEM((rows, slots), BF16),
-            pltpu.SemaphoreType.DMA((4,)),
+            pltpu.VMEM((rows, w_out.shape[1]), BF16),
+            pltpu.SemaphoreType.DMA((3,)),
+            pltpu.SemaphoreType.DMA((features // 256,)),
+            pltpu.SemaphoreType.DMA((w_out.shape[1] // 256,)),
             pltpu.SemaphoreType.DMA((2,)),
             pltpu.SemaphoreType.DMA((2,)),
             pltpu.SemaphoreType.DMA((n,)),

time: 122 us -> 120 us (0.984)
  no operation moved by 1% of the time
where the time goes in v2:
time: 120 us
  Pallas kernels  116 us (97%)
  local copies, waits for them, and re-layouts  3.65 us (3%)
    pallas_call x1, Pallas kernels, per_device(): pl.pallas_call(functools.partial(kernel, n), out_shape=jax.ShapeDtypeStru...  116 us
    unnamed x5, local copies, waits for them, and re-layouts  3.57 us

profile of v2, /device:TPU:5, one launch (start us, length us, event | category | flops | bytes accessed | tf_op | source)
XLA Modules:
  0.0 120.2 jit_solution(16954009559052633720)
XLA Ops:
  0.0 0.1 pad.3.clone
  0.1 0.8 add_convert_fusion.info_ref
  0.9 0.0 copy-start
  0.9 1.6 %copy-done = bf16[512,2048]{1,0:T(8,128)(2,1)S(1)} copy-done((bf16[512,2048]{1,0:T(8,128)(2,1)S(1)}, bf16[512,2048]{1,0:T(8,128)(2,1)}, u32[]{:S(2)}) %copy-start) | copy-done | bytes 2097176
  2.5 0.0 copy-start.1
  2.5 0.7 copy-done.1
  3.1 115.7 %shard_map.82 = bf16[512,2048]{1,0:T(8,128)(2,1)S(1)} custom-call(f32[8]{0:T(128)S(1)} %copy-done.1, f32[8,512]{1,0:T(8,128)S(1)} %add_convert_fusion.info_ref, bf16[512,2048]{1,0:T(8,128)(2,1)S(1)} %copy-done, bf16[2048,1024]{1,0:T(8,128)(2,1)} %wq_hbm.1, bf16[1024,2048]{1,0:T(8,128)(2,1)} %wo_hbm.1, bf16[2,4,128,1024]{3,2,1,0:T(8,128)(2,1)} %kv_hbm.1), custom_call_target="tpu_custom_call" | custom-call | flops 12000000000 | bytes 16777216 | tf_op jit(solution)/shard_map/pallas_call | solution.py:328
  118.8 1.3 %copy.10 = bf16[512,2048]{1,0:T(8,128)(2,1)} copy(bf16[512,2048]{1,0:T(8,128)(2,1)S(1)} %shard_map.82) | data formatting | bytes 4194304
  (1 shorter events, 0.0 us)
Async XLA Ops:
  0.9 1.6 %copy-start = (bf16[512,2048]{1,0:T(8,128)(2,1)S(1)}, bf16[512,2048]{1,0:T(8,128)(2,1)}, u32[]{:S(2)}) copy-start(bf16[512,2048]{1,0:T(8,128)(2,1)} %x_hbm.1) | copy-start | bytes 6291460
  2.5 0.7 copy-start.1
